TPU v7x, 32 devices: a whole 2x2x4 slice. The times are simulated.
32 devices in a mesh: groups: 2 (over x), ep: 16 (over z, y, core).
Axes of the slice: x: 2, y: 2, z: 4, core: 2. Of those that a mesh axis runs over, the one named last changes fastest.
Arguments:
- resid: bfloat16 [128, 3584], P(('groups', 'ep')), parts along dimension 0, may hold values from -45 to 45
- q_latent: bfloat16 [128, 16, 512], P(('groups', 'ep')), parts along dimension 0, may hold values from -500 to 500
- q_rope: bfloat16 [128, 16, 64], P(('groups', 'ep')), parts along dimension 0, may hold values from -6 to 6
- cache_latent: bfloat16 [128, 1024, 512], P(('groups', 'ep')), parts along dimension 0, may hold values from -4 to 4
- cache_rope: bfloat16 [128, 64, 1024], P(('groups', 'ep')), parts along dimension 0, may hold values from -4 to 4
- lengths: int32 [128], P(('groups', 'ep')), parts along dimension 0, may hold values from 2 to 1024, as said below
- w_value: bfloat16 [16, 512, 128], P('ep'), may hold values from -0.25 to 0.25
- w_out: bfloat16 [2048, 3584], P('ep'), may hold values from -0.125 to 0.125
- norm_gain: float32 [3584], replicated, may hold values from 0.1 to 1.9
- routes: int32 [128, 8], P(('groups', 'ep')), parts along dimension 0, may hold values from 0 to 15, all different within a row; in each aligned block of 4 rows (0 to 3, 4 to 7, ...) at most 2 rows name the same one
- route_scores: float32 [128, 8], P(('groups', 'ep')), parts along dimension 0, may hold values from 0.05 to 1
- placement: int32 [32], P('groups'), parts along dimension 0, may hold values from 0 to 15, each once
- w_gate: bfloat16 [16384, 3584], P('ep'), may hold values from -0.09375 to 0.09375
- w_up: bfloat16 [16384, 3584], P('ep'), may hold values from -0.09375 to 0.09375
- w_down: bfloat16 [16384, 3584], P('ep'), may hold values from -0.1875 to 0.1875
Outputs:
- mixed: bfloat16 [128, 3584], P(('groups', 'ep')), parts along dimension 0
There are 2 independent parts, one for each index of `groups`. A program takes and returns all parts, laid end to end along the dimension named above; an argument that names none is the same for every part. Nothing has to cross between parts.
Inputs may be any that keep to these rules, and one draw needn't show every extreme that they name: `routes`: each row names 8 different experts; in the rows of one device (aligned blocks of 4 rows) every expert is named by exactly 2 rows. `placement`: each expert has its own slot. Positions 0 to lengths[r] - 1 of row r are live; some row is live over all 1024 positions.
All inputs are finite; a program needn't handle non-finite values.
Results may differ from a plain program's by a relative error of at most 0.0045.
Values may be sent and summed in bfloat16 or wider, within the bound.
A program may use at most 128 MiB of HBM per device.

v0:
```python
import jax
import jax.numpy as jnp
from jax import lax
from jax.sharding import PartitionSpec as P


def normalize(hidden, norm_gain):
    mean_sq = jnp.mean(hidden * hidden, axis=-1, keepdims=True)
    return (hidden * lax.rsqrt(mean_sq + 1e-06) * norm_gain).astype(jnp.bfloat16)


def local(
    resid,
    q_latent,
    q_rope,
    cache_latent,
    cache_rope,
    lengths,
    w_value,
    w_out,
    norm_gain,
    routes,
    route_scores,
    placement,
    w_gate,
    w_up,
    w_down,
):
    devices = lax.axis_size("ep")
    rows_dev = resid.shape[0]
    width = resid.shape[1]
    length = cache_latent.shape[1]
    experts = placement.shape[0]
    top_count = routes.shape[1]
    cap = rows_dev * top_count // experts
    shards = devices // experts
    scale = (w_value.shape[2] + q_rope.shape[2]) ** (-0.5)
    scores = jnp.einsum("rhc,rpc->rhp", q_latent, cache_latent, preferred_element_type=jnp.float32)
    scores = scores + jnp.einsum(
        "rhk,rkp->rhp", q_rope, cache_rope, preferred_element_type=jnp.float32
    )
    scores = scores * scale
    valid = jnp.arange(length, dtype=jnp.int32)[None, None, :] < lengths[:, None, None]
    scores = jnp.where(valid, scores, -1e30)
    top = jnp.max(scores, axis=-1, keepdims=True)
    expo = jnp.where(valid, jnp.exp(scores - top), 0.0)
    probs = (expo / jnp.sum(expo, axis=-1, keepdims=True)).astype(jnp.bfloat16)
    o_local = jnp.einsum(
        "rhp,rpc->rhc", probs, cache_latent, preferred_element_type=jnp.float32
    ).astype(jnp.bfloat16)
    o_heads = lax.all_to_all(o_local, "ep", split_axis=1, concat_axis=0, tiled=True)
    values = jnp.einsum(
        "rhc,hcv->rhv", o_heads, w_value, preferred_element_type=jnp.float32
    ).astype(jnp.bfloat16)
    flat = values.reshape(values.shape[0], -1)
    expert_ids = jnp.arange(experts, dtype=jnp.int32)
    slot_of_dev = jnp.arange(devices, dtype=jnp.int32) // shards
    dev_expert = (placement[None, :] == slot_of_dev[:, None]).astype(jnp.float32)
    chosen = routes[:, :, None] == expert_ids[None, None, :]
    member = jnp.any(chosen, axis=1).astype(jnp.int32)
    weights = 2.5 * route_scores / jnp.sum(route_scores, axis=-1, keepdims=True)
    weight_expert = jnp.sum(jnp.where(chosen, weights[:, :, None], 0.0), axis=1)
    rank_rows = jnp.cumsum(member, axis=0) - member
    slots = jnp.arange(cap, dtype=jnp.int32)
    pick = (member.T[:, None, :] == 1) & (rank_rows.T[:, None, :] == slots[None, :, None])
    send_map = jnp.einsum("de,ecr->dcr", dev_expert, pick.astype(jnp.float32))
    attn = lax.psum_scatter(
        jnp.dot(flat, w_out, preferred_element_type=jnp.float32),
        "ep",
        scatter_dimension=0,
        tiled=True,
    )
    hidden = resid.astype(jnp.float32) + attn
    normed = normalize(hidden, norm_gain)
    outgoing = jnp.einsum(
        "dcr,rw->dcw", send_map.astype(jnp.bfloat16), normed, preferred_element_type=jnp.float32
    ).astype(jnp.bfloat16)
    incoming = lax.all_to_all(outgoing, "ep", split_axis=0, concat_axis=0, tiled=True)
    taken = incoming.reshape(-1, width)
    dims = (((1,), (1,)), ((), ()))
    gate = lax.dot_general(taken, w_gate, dims, preferred_element_type=jnp.float32)
    up = lax.dot_general(taken, w_up, dims, preferred_element_type=jnp.float32)
    act = (jax.nn.silu(gate) * up).astype(jnp.bfloat16)
    weight_dev = jnp.dot(weight_expert, dev_expert.T, precision=lax.Precision.HIGHEST)
    combine_weights = jnp.transpose(send_map, (2, 0, 1)) * weight_dev[:, :, None]
    part_out = jnp.dot(act, w_down, preferred_element_type=jnp.float32).reshape(devices, cap, width)
    returned = lax.all_to_all(
        part_out.astype(jnp.bfloat16), "ep", split_axis=0, concat_axis=0, tiled=True
    ).astype(part_out.dtype)
    moe = jnp.einsum("rdc,dcw->rw", combine_weights, returned, precision=lax.Precision.HIGHEST)
    return (hidden + moe).astype(jnp.bfloat16)


def solution(mesh):
    return jax.shard_map(
        local,
        mesh=mesh,
        in_specs=(
            P(("groups", "ep"), None),
            P(("groups", "ep"), None, None),
            P(("groups", "ep"), None, None),
            P(("groups", "ep"), None, None),
            P(("groups", "ep"), None, None),
            P(("groups", "ep")),
            P("ep", None, None),
            P("ep", None),
            P(),
            P(("groups", "ep"), None),
            P(("groups", "ep"), None),
            P("groups"),
            P("ep", None),
            P("ep", None),
            P("ep", None),
        ),
        out_specs=P(("groups", "ep"), None),
        check_vma=False,
    )
```

profile of v0, /device:TPU:0, one launch (start us, length us, event | category | flops | bytes accessed | tf_op | source)
XLA Modules:
  0.0 175.3 jit_solution(10206663656031448534)
XLA Ops:
  6.5 0.0 copy-start
  6.5 0.0 copy-start.7
  6.5 0.0 copy-start.4
  6.5 0.0 copy-start.1
  6.5 0.0 copy-start.6
  6.5 0.0 copy-start.2
  6.6 0.0 copy-start.3
  6.6 0.8 iota_compare_fusion.1
  7.4 0.0 copy-start.5
  7.4 3.4 %fusion.38 = f32[4,16,1024]{2,1,0:T(8,128)S(1)} fusion(bf16[4,16,512]{2,1,0:T(8,128)(2,1)} %param.16, bf16[4,1024,512]{2,1,0:T(8,128)(2,1)} %param.18), kind=kOutput, calls=%fused_computation.56 | convolution fusion | flops 67108864 | bytes 4521984 | tf_op jit(solution)/shard_map/rhc,rpc->rhp/dot_general | solution.py:38
  10.8 1.3 fusion.7
  12.1 0.2 fusion.37
  12.3 2.9 %convolution_convert_fusion.2 = bf16[4,16,512]{2,1,0:T(8,128)(2,1)S(1)} fusion(bf16[4,1024,512]{2,1,0:T(8,128)(2,1)} %param.18, f32[4,16]{1,0:T(4,128)S(1)} %fusion.37, f32[4,16,1024]{2,1,0:T(8,128)S(1)} %fusion.7, pred[4,1024]{1,0:T(4,128)(4,1)S(1)} %iota_compare_fusion.1), kind=kOutput, calls=%fused_computation.14 | convolution fusion | flops 67404864 | bytes 4526336 | tf_op jit(solution)/shard_map/rhp,rpc->rhc/dot_general | solution.py:48
  15.2 0.7 copy.23
  15.9 7.4 %all-to-all-start = ((bf16[4,16,512]{2,0,1:T(4,128)(2,1)}), bf16[4,16,512]{2,0,1:T(4,128)(2,1)S(1)}, u32[]{:S(2)}, u32[]{:S(2)}) async-start(bf16[4,16,512]{2,0,1:T(4,128)(2,1)} %copy.23), calls=%async_computation | async-start | bytes 131072 | tf_op jit(solution)/shard_map/all_to_all | solution.py:51
  23.3 0.0 all-reduce.3.cloned.1.call-start
  23.3 0.0 copy-done.4
  23.3 0.1 fusion.24
  23.5 6.7 %all-to-all-done = bf16[4,16,512]{2,0,1:T(4,128)(2,1)S(1)} async-done(((bf16[4,16,512]{2,0,1:T(4,128)(2,1)}), bf16[4,16,512]{2,0,1:T(4,128)(2,1)S(1)}, u32[]{:S(2)}, u32[]{:S(2)}) %all-to-all-start) | async-done | bytes 65568 | tf_op jit(solution)/shard_map/all_to_all | solution.py:51
  30.2 0.0 copy-done
  30.2 0.0 copy-done.1
  30.2 1.4 fusion.9
  31.6 0.0 all-reduce.3.cloned.1.call-update
  31.6 0.0 copy-done.7
  31.7 0.6 dynamic-slice
  32.9 0.0 copy-done.6
  32.9 0.1 fusion.26
  33.0 88.0 %all-reduce.3.cloned.1.call-done = f32[64,3584]{1,0:T(8,128)} async-done(((f32[64,3584]{1,0:T(8,128)}), f32[64,3584]{1,0:T(8,128)}) %all-reduce.3.cloned.1.call-update) | async-done | bytes 917520
  121.0 0.0 copy-done.2
  121.0 1.0 multiply_reduce_fusion
  122.1 0.0 copy-done.3
  122.1 1.2 convolution_convert_fusion.1
  123.3 0.9 copy.24
  124.2 5.0 %all-to-all-start.1 = ((bf16[16,2,3584]{2,1,0:T(2,128)(2,1)}), bf16[16,2,3584]{2,1,0:T(2,128)(2,1)S(1)}, u32[]{:S(2)}, u32[]{:S(2)}) async-start(bf16[16,2,3584]{2,1,0:T(2,128)(2,1)} %copy.24), calls=%async_computation.1 | async-start | bytes 458752 | tf_op jit(solution)/shard_map/all_to_all | solution.py:78
  129.3 0.0 copy-done.5
  129.3 0.1 reduce_sum.37
  129.4 9.4 %all-to-all-done.1 = bf16[16,2,3584]{2,1,0:T(2,128)(2,1)S(1)} async-done(((bf16[16,2,3584]{2,1,0:T(2,128)(2,1)}), bf16[16,2,3584]{2,1,0:T(2,128)(2,1)S(1)}, u32[]{:S(2)}, u32[]{:S(2)}) %all-to-all-start.1) | async-done | bytes 229408 | tf_op jit(solution)/shard_map/all_to_all | solution.py:78
  138.8 0.1 reshape.58
  138.9 5.3 %fusion.39 = f32[32,1024]{1,0:T(8,128)S(1)} fusion(bf16[32,3584]{1,0:T(8,128)(2,1)S(1)} %reshape.58, bf16[1024,3584]{1,0:T(8,128)(2,1)} %param.27), kind=kOutput, calls=%fused_computation.57 | convolution fusion | flops 234881024 | bytes 7700480 | tf_op jit(solution)/shard_map/dot_general | solution.py:81
  144.2 8.7 %convolution_convert_fusion = bf16[32,3584]{1,0:T(8,128)(2,1)S(1)} fusion(bf16[1024,3584]{1,0:T(8,128)(2,1)} %param.29, bf16[32,3584]{1,0:T(8,128)(2,1)S(1)} %reshape.58, bf16[1024,3584]{1,0:T(8,128)(2,1)} %param.28, f32[32,1024]{1,0:T(8,128)S(1)} %fusion.39), kind=kOutput, calls=%fused_computation.1 | convolution fusion | flops 470073344 | bytes 15269888 | tf_op jit(solution)/shard_map/dot_general | solution.py:86
  152.9 0.8 convert_element_type.55
  153.7 3.5 %all-to-all-start.2 = ((bf16[16,2,3584]{2,1,0:T(2,128)(2,1)}), bf16[16,2,3584]{2,1,0:T(2,128)(2,1)S(1)}, u32[]{:S(2)}, u32[]{:S(2)}) async-start(bf16[16,2,3584]{2,1,0:T(2,128)(2,1)} %convert_element_type.55), calls=%async_computation.2 | async-start | bytes 458752 | tf_op jit(solution)/shard_map/all_to_all | solution.py:87
  157.2 0.1 multiply_divide_fusion
  157.3 0.1 select_reduce_fusion
  157.4 0.1 fusion.25
  157.5 9.2 %all-to-all-done.2 = bf16[16,2,3584]{2,1,0:T(2,128)(2,1)S(1)} async-done(((bf16[16,2,3584]{2,1,0:T(2,128)(2,1)}), bf16[16,2,3584]{2,1,0:T(2,128)(2,1)S(1)}, u32[]{:S(2)}, u32[]{:S(2)}) %all-to-all-start.2) | async-done | bytes 229408 | tf_op jit(solution)/shard_map/all_to_all | solution.py:87
  166.7 1.8 %fusion.2 = bf16[4,3584]{1,0:T(4,128)(2,1)} fusion(bf16[16,2,3584]{2,1,0:T(2,128)(2,1)S(1)} %all-to-all-done.2, f32[4,16,2]{1,0,2:T(4,128)S(1)} %bitcast.45, f32[4,16]{1,0:T(4,128)S(1)} %fusion.25, f32[64,3584]{1,0:T(8,128)} %all-reduce.3.cloned.1.call-done, u32[]{:T(128)S(6)} %multiply.7, bf16[4,3584]{1,0:T(4,128)(2,1)S(1)} %copy-done.2), kind=kOutput, calls=%fused_computation.5 | convolution fusion | flops 5562496 | bytes 344836 | tf_op jit(solution)/shard_map/rdc,dcw->rw/dot_general | solution.py:90
  (6 shorter events, 0.1 us)
Async XLA Ops:
  6.5 23.7 %copy-start = (bf16[128,3584]{1,0:T(8,128)(2,1)S(1)}, bf16[128,3584]{1,0:T(8,128)(2,1)}, u32[]{:S(2)}) copy-start(bf16[128,3584]{1,0:T(8,128)(2,1)} %param.22) | copy-start | bytes 2752516
  6.5 25.1 %copy-start.7 = (u32[32]{0:T(128)S(1)}, u32[32]{0:T(128)}, u32[]{:S(2)}) copy-start(u32[32]{0:T(128)} %constant.48) | copy-start | bytes 388
  6.5 16.8 %copy-start.4 = (s32[4,8]{1,0:T(4,128)S(1)}, s32[4,8]{1,0:T(4,128)}, u32[]{:S(2)}) copy-start(s32[4,8]{1,0:T(4,128)} %param.24) | copy-start | bytes 388
  6.5 23.7 %copy-start.1 = (bf16[1,512,128]{2,1,0:T(8,128)(2,1)S(1)}, bf16[1,512,128]{2,1,0:T(8,128)(2,1)}, u32[]{:S(2)}) copy-start(bf16[1,512,128]{2,1,0:T(8,128)(2,1)} %param.21) | copy-start | bytes 393220
  6.5 26.4 %copy-start.6 = (s32[16]{0:T(128)S(1)}, s32[16]{0:T(128)}, u32[]{:S(2)}) copy-start(s32[16]{0:T(128)} %param.26) | copy-start | bytes 196
  6.5 114.5 %copy-start.2 = (bf16[4,3584]{1,0:T(4,128)(2,1)S(1)}, bf16[4,3584]{1,0:T(4,128)(2,1)}, u32[]{:S(2)}) copy-start(bf16[4,3584]{1,0:T(4,128)(2,1)} %param.15) | copy-start | bytes 86020
  6.6 115.5 %copy-start.3 = (f32[3584]{0:T(1024)S(1)}, f32[3584]{0:T(1024)}, u32[]{:S(2)}) copy-start(f32[3584]{0:T(1024)} %param.23) | copy-start | bytes 43012
  7.4 121.9 %copy-start.5 = (f32[4,8]{1,0:T(4,128)S(1)}, f32[4,8]{1,0:T(4,128)}, u32[]{:S(2)}) copy-start(f32[4,8]{1,0:T(4,128)} %param.25) | copy-start | bytes 388
  15.9 14.3 %all-to-all-start = ((bf16[4,16,512]{2,0,1:T(4,128)(2,1)}), bf16[4,16,512]{2,0,1:T(4,128)(2,1)S(1)}, u32[]{:S(2)}, u32[]{:S(2)}) async-start(bf16[4,16,512]{2,0,1:T(4,128)(2,1)} %copy.23), calls=%async_computation | async-start | bytes 131072 | tf_op jit(solution)/shard_map/all_to_all | solution.py:51
  23.3 97.8 %all-reduce.3.cloned.1.call-start = ((), (), s32[]{:S(2)}) async-start(), calls=%async_computation.3 | async-start | bytes 1835008
  124.2 14.5 %all-to-all-start.1 = ((bf16[16,2,3584]{2,1,0:T(2,128)(2,1)}), bf16[16,2,3584]{2,1,0:T(2,128)(2,1)S(1)}, u32[]{:S(2)}, u32[]{:S(2)}) async-start(bf16[16,2,3584]{2,1,0:T(2,128)(2,1)} %copy.24), calls=%async_computation.1 | async-start | bytes 458752 | tf_op jit(solution)/shard_map/all_to_all | solution.py:78
  153.7 13.0 %all-to-all-start.2 = ((bf16[16,2,3584]{2,1,0:T(2,128)(2,1)}), bf16[16,2,3584]{2,1,0:T(2,128)(2,1)S(1)}, u32[]{:S(2)}, u32[]{:S(2)}) async-start(bf16[16,2,3584]{2,1,0:T(2,128)(2,1)} %convert_element_type.55), calls=%async_computation.2 | async-start | bytes 458752 | tf_op jit(solution)/shard_map/all_to_all | solution.py:87
Sparse Core Ops, SparseCore 0:
  31.8 89.2 all-reduce.2
where the time goes:
time: 176 us; the launch traced here: 175 us
  waiting for transfers between devices  113 us (64%)
  matrix products  26.2 us (15%)
  starting transfers between devices  16 us (9%)
  between operations  14.2 us (8%)
  local copies, waits for them, and re-layouts  3.12 us (2%)
  other arithmetic  2.51 us (1%)
    unnamed x2, waiting for transfers between devices  88 us
    all_to_all x1, waiting for transfers between devices, local(): lax.all_to_all(outgoing, 'ep', split_axis=0, concat_axis=0, tiled=True)  9.39 us
    all_to_all x1, waiting for transfers between devices, local(): lax.all_to_all(part_out.astype(jnp.bfloat16), 'ep', split_axis=0, concat_...  9.19 us
    dot_general x1, matrix products, local(): jnp.dot(act, w_down, preferred_element_type=jnp.float32)  8.69 us
    all_to_all x1, starting transfers between devices, local(): lax.all_to_all(o_local, 'ep', split_axis=1, concat_axis=0, tiled=True)  7.39 us
    all_to_all x1, waiting for transfers between devices, local(): lax.all_to_all(o_local, 'ep', split_axis=1, concat_axis=0, tiled=True)  6.7 us
    dot_general x1, matrix products, local(): lax.dot_general(taken, w_gate, dims, preferred_element_type=jnp.float32)  5.3 us
    all_to_all x1, starting transfers between devices, local(): lax.all_to_all(outgoing, 'ep', split_axis=0, concat_axis=0, tiled=True)  5.02 us
  transfers between devices with their start and end apart: 4, of which 4 were waited for; matrix products, arithmetic and copies ran while one was open for 1% of the time, Pallas kernels for 0%

commit v1 on v0

--- a/solution.py
+++ b/solution.py
@@ -64,12 +64,10 @@
     slots = jnp.arange(cap, dtype=jnp.int32)
     pick = (member.T[:, None, :] == 1) & (rank_rows.T[:, None, :] == slots[None, :, None])
     send_map = jnp.einsum("de,ecr->dcr", dev_expert, pick.astype(jnp.float32))
-    attn = lax.psum_scatter(
-        jnp.dot(flat, w_out, preferred_element_type=jnp.float32),
-        "ep",
-        scatter_dimension=0,
-        tiled=True,
-    )
+    partial = jnp.dot(flat, w_out, preferred_element_type=jnp.float32)
+    partial = partial.astype(jnp.bfloat16).reshape(devices, rows_dev, width)
+    shares = lax.all_to_all(partial, "ep", split_axis=0, concat_axis=0, tiled=True)
+    attn = jnp.sum(shares.astype(jnp.float32), axis=0)
     hidden = resid.astype(jnp.float32) + attn
     normed = normalize(hidden, norm_gain)
     outgoing = jnp.einsum(

time: 176 us -> 86 us (0.49)
  waiting for transfers between devices: 113 us -> 38.4 us
  between operations: 14.2 us -> 0.14 us
  matrix products: 26.2 us -> 23.4 us
  starting transfers between devices: 16 us -> 18.3 us
    unnamed x2 -> x0, waiting for transfers between devices: 88 us -> none
    all_to_all x0 -> x1, waiting for transfers between devices: none -> 13 us  [local(): lax.all_to_all(partial, 'ep', split_axis=0, concat_axis=0, tiled=True)]
    all_to_all x0 -> x1, starting transfers between devices: none -> 3.56 us  [local(): lax.all_to_all(partial, 'ep', split_axis=0, concat_axis=0, tiled=True)]
where the time goes in v1:
time: 86 us; the launch traced here: 85.4 us
  waiting for transfers between devices  38.4 us (45%)
  matrix products  23.4 us (27%)
  starting transfers between devices  18.3 us (21%)
  local copies, waits for them, and re-layouts  3.38 us (4%)
  other arithmetic  1.82 us (2%)
    all_to_all x1, waiting for transfers between devices, local(): lax.all_to_all(partial, 'ep', split_axis=0, concat_axis=0, tiled=True)  13 us
    all_to_all x1, waiting for transfers between devices, local(): lax.all_to_all(outgoing, 'ep', split_axis=0, concat_axis=0, tiled=True)  9.39 us
    all_to_all x1, waiting for transfers between devices, local(): lax.all_to_all(part_out.astype(jnp.bfloat16), 'ep', split_axis=0, concat_...  9.19 us
    dot_general x1, matrix products, local(): jnp.dot(act, w_down, preferred_element_type=jnp.float32)  8.69 us
    all_to_all x1, starting transfers between devices, local(): lax.all_to_all(o_local, 'ep', split_axis=1, concat_axis=0, tiled=True)  7.39 us
    all_to_all x1, waiting for transfers between devices, local(): lax.all_to_all(o_local, 'ep', split_axis=1, concat_axis=0, tiled=True)  6.8 us
    dot_general x1, matrix products, local(): lax.dot_general(taken, w_gate, dims, preferred_element_type=jnp.float32)  5.29 us
    all_to_all x1, starting transfers between devices, local(): lax.all_to_all(outgoing, 'ep', split_axis=0, concat_axis=0, tiled=True)  3.81 us
  transfers between devices with their start and end apart: 4, of which 4 were waited for; matrix products, arithmetic and copies ran while one was open for 1% of the time, Pallas kernels for 0%

profile of v1, /device:TPU:0, one launch (start us, length us, event | category | flops | bytes accessed | tf_op | source)
XLA Modules:
  0.0 85.4 jit_solution(13820745567113178809)
XLA Ops:
  0.0 0.0 copy-start
  0.0 0.0 copy-start.4
  0.0 0.0 copy-start.2
  0.0 0.0 copy-start.6
  0.0 0.8 iota_compare_fusion.1
  0.8 0.0 copy-start.1
  0.8 0.0 copy-start.3
  0.8 0.0 copy-start.5
  0.9 3.4 %fusion.36 = f32[4,16,1024]{2,1,0:T(8,128)S(1)} fusion(bf16[4,16,512]{2,1,0:T(8,128)(2,1)} %param.16, bf16[4,1024,512]{2,1,0:T(8,128)(2,1)} %param.18), kind=kOutput, calls=%fused_computation.56 | convolution fusion | flops 67108864 | bytes 4521984 | tf_op jit(solution)/shard_map/rhc,rpc->rhp/dot_general | solution.py:38
  4.3 1.3 %fusion.7 = f32[4,16,1024]{2,1,0:T(8,128)S(1)} fusion(f32[4,16,1024]{2,1,0:T(8,128)S(1)} %fusion.36, bf16[4,16,64]{2,1,0:T(8,128)(2,1)} %param.17, bf16[4,64,1024]{2,1,0:T(8,128)(2,1)} %param.19, pred[4,1024]{1,0:T(4,128)(4,1)S(1)} %iota_compare_fusion.1), kind=kOutput, calls=%fused_computation.12 | convolution fusion | flops 8585216 | bytes 1060864 | tf_op jit(solution)/shard_map/rhk,rkp->rhp/dot_general | solution.py:39
  5.6 0.2 fusion.35
  5.8 2.9 %convolution_convert_fusion.3 = bf16[4,16,512]{2,1,0:T(8,128)(2,1)S(1)} fusion(bf16[4,1024,512]{2,1,0:T(8,128)(2,1)} %param.18, f32[4,16]{1,0:T(4,128)S(1)} %fusion.35, f32[4,16,1024]{2,1,0:T(8,128)S(1)} %fusion.7, pred[4,1024]{1,0:T(4,128)(4,1)S(1)} %iota_compare_fusion.1), kind=kOutput, calls=%fused_computation.15 | convolution fusion | flops 67404864 | bytes 4526336 | tf_op jit(solution)/shard_map/rhp,rpc->rhc/dot_general | solution.py:48
  8.7 0.7 copy.23
  9.4 7.4 %all-to-all-start = ((bf16[4,16,512]{2,0,1:T(4,128)(2,1)}), bf16[4,16,512]{2,0,1:T(4,128)(2,1)S(1)}, u32[]{:S(2)}, u32[]{:S(2)}) async-start(bf16[4,16,512]{2,0,1:T(4,128)(2,1)} %copy.23), calls=%async_computation | async-start | bytes 131072 | tf_op jit(solution)/shard_map/all_to_all | solution.py:51
  16.8 0.0 copy-done.4
  16.8 0.1 fusion.23
  16.9 6.8 %all-to-all-done = bf16[4,16,512]{2,0,1:T(4,128)(2,1)S(1)} async-done(((bf16[4,16,512]{2,0,1:T(4,128)(2,1)}), bf16[4,16,512]{2,0,1:T(4,128)(2,1)S(1)}, u32[]{:S(2)}, u32[]{:S(2)}) %all-to-all-start) | async-done | bytes 65568 | tf_op jit(solution)/shard_map/all_to_all | solution.py:51
  23.7 0.0 copy-done
  23.7 0.0 copy-done.2
  23.7 0.4 convolution_convert_fusion
  24.1 0.9 %reshape.61 = bf16[16,4,3584]{2,1,0:T(4,128)(2,1)} reshape(bf16[64,3584]{1,0:T(8,128)(2,1)S(1)} %convolution_convert_fusion) | data formatting | bytes 917504 | tf_op jit(solution)/shard_map/reshape | solution.py:68
  25.0 3.6 %all-to-all-start.1 = ((bf16[16,4,3584]{2,1,0:T(4,128)(2,1)}), bf16[16,4,3584]{2,1,0:T(4,128)(2,1)S(1)}, u32[]{:S(2)}, u32[]{:S(2)}) async-start(bf16[16,4,3584]{2,1,0:T(4,128)(2,1)} %reshape.61), calls=%async_computation.1 | async-start | bytes 917504 | tf_op jit(solution)/shard_map/all_to_all | solution.py:69
  28.6 0.0 copy-done.6
  28.7 0.1 fusion.25
  28.8 13.0 %all-to-all-done.1 = bf16[16,4,3584]{2,1,0:T(4,128)(2,1)S(1)} async-done(((bf16[16,4,3584]{2,1,0:T(4,128)(2,1)}), bf16[16,4,3584]{2,1,0:T(4,128)(2,1)S(1)}, u32[]{:S(2)}, u32[]{:S(2)}) %all-to-all-start.1) | async-done | bytes 458784 | tf_op jit(solution)/shard_map/all_to_all | solution.py:69
  41.8 0.2 convert_reduce_fusion
  42.0 0.0 copy-done.1
  42.0 0.1 multiply_reduce_fusion
  42.1 0.0 copy-done.3
  42.1 0.3 convolution_convert_fusion.2
  42.4 0.9 %copy.24 = bf16[16,2,3584]{2,1,0:T(2,128)(2,1)} copy(bf16[16,2,3584]{2,0,1:T(8,128)(2,1)S(1)} %convolution_convert_fusion.2) | data formatting | bytes 458752 | tf_op jit(solution)/shard_map/convert_element_type | solution.py:75
  43.3 3.8 %all-to-all-start.2 = ((bf16[16,2,3584]{2,1,0:T(2,128)(2,1)}), bf16[16,2,3584]{2,1,0:T(2,128)(2,1)S(1)}, u32[]{:S(2)}, u32[]{:S(2)}) async-start(bf16[16,2,3584]{2,1,0:T(2,128)(2,1)} %copy.24), calls=%async_computation.2 | async-start | bytes 458752 | tf_op jit(solution)/shard_map/all_to_all | solution.py:76
  47.2 0.0 copy-done.5
  47.2 0.1 reduce_sum.47
  47.3 9.4 %all-to-all-done.2 = bf16[16,2,3584]{2,1,0:T(2,128)(2,1)S(1)} async-done(((bf16[16,2,3584]{2,1,0:T(2,128)(2,1)}), bf16[16,2,3584]{2,1,0:T(2,128)(2,1)S(1)}, u32[]{:S(2)}, u32[]{:S(2)}) %all-to-all-start.2) | async-done | bytes 229408 | tf_op jit(solution)/shard_map/all_to_all | solution.py:76
  56.7 0.1 reshape.62
  56.8 5.3 %fusion.37 = f32[32,1024]{1,0:T(8,128)S(1)} fusion(bf16[32,3584]{1,0:T(8,128)(2,1)S(1)} %reshape.62, bf16[1024,3584]{1,0:T(8,128)(2,1)} %param.27), kind=kOutput, calls=%fused_computation.57 | convolution fusion | flops 234881024 | bytes 7700480 | tf_op jit(solution)/shard_map/dot_general | solution.py:79
  62.1 8.7 %convolution_convert_fusion.1 = bf16[32,3584]{1,0:T(8,128)(2,1)S(1)} fusion(bf16[1024,3584]{1,0:T(8,128)(2,1)} %param.29, bf16[32,3584]{1,0:T(8,128)(2,1)S(1)} %reshape.62, bf16[1024,3584]{1,0:T(8,128)(2,1)} %param.28, f32[32,1024]{1,0:T(8,128)S(1)} %fusion.37), kind=kOutput, calls=%fused_computation.2 | convolution fusion | flops 470073344 | bytes 15269888 | tf_op jit(solution)/shard_map/dot_general | solution.py:84
  70.8 0.8 convert_element_type.63
  71.5 3.5 %all-to-all-start.3 = ((bf16[16,2,3584]{2,1,0:T(2,128)(2,1)}), bf16[16,2,3584]{2,1,0:T(2,128)(2,1)S(1)}, u32[]{:S(2)}, u32[]{:S(2)}) async-start(bf16[16,2,3584]{2,1,0:T(2,128)(2,1)} %convert_element_type.63), calls=%async_computation.3 | async-start | bytes 458752 | tf_op jit(solution)/shard_map/all_to_all | solution.py:85
  75.1 0.1 multiply_divide_fusion
  75.1 0.1 select_reduce_fusion
  75.2 0.1 fusion.24
  75.4 9.2 %all-to-all-done.3 = bf16[16,2,3584]{2,1,0:T(2,128)(2,1)S(1)} async-done(((bf16[16,2,3584]{2,1,0:T(2,128)(2,1)}), bf16[16,2,3584]{2,1,0:T(2,128)(2,1)S(1)}, u32[]{:S(2)}, u32[]{:S(2)}) %all-to-all-start.3) | async-done | bytes 229408 | tf_op jit(solution)/shard_map/all_to_all | solution.py:85
  84.5 0.9 %fusion.2 = bf16[4,3584]{1,0:T(4,128)(2,1)} fusion(bf16[16,2,3584]{2,1,0:T(2,128)(2,1)S(1)} %all-to-all-done.3, f32[4,3584]{1,0:T(4,128)S(1)} %convert_reduce_fusion, bf16[4,3584]{1,0:T(4,128)(2,1)S(1)} %copy-done.1, f32[4,16,2]{1,0,2:T(4,128)S(1)} %bitcast.44, f32[4,16]{1,0:T(4,128)S(1)} %fusion.24), kind=kOutput, calls=%fused_computation.6 | convolution fusion | flops 5562496 | bytes 344832 | tf_op jit(solution)/shard_map/rdc,dcw->rw/dot_general | solution.py:88
  (6 shorter events, 0.1 us)
Async XLA Ops:
  0.0 23.7 %copy-start = (bf16[128,3584]{1,0:T(8,128)(2,1)S(1)}, bf16[128,3584]{1,0:T(8,128)(2,1)}, u32[]{:S(2)}) copy-start(bf16[128,3584]{1,0:T(8,128)(2,1)} %param.22) | copy-start | bytes 2752516
  0.0 16.8 %copy-start.4 = (s32[4,8]{1,0:T(4,128)S(1)}, s32[4,8]{1,0:T(4,128)}, u32[]{:S(2)}) copy-start(s32[4,8]{1,0:T(4,128)} %param.24) | copy-start | bytes 388
  0.0 23.7 %copy-start.2 = (bf16[1,512,128]{2,1,0:T(8,128)(2,1)S(1)}, bf16[1,512,128]{2,1,0:T(8,128)(2,1)}, u32[]{:S(2)}) copy-start(bf16[1,512,128]{2,1,0:T(8,128)(2,1)} %param.21) | copy-start | bytes 393220
  0.0 28.6 %copy-start.6 = (s32[16]{0:T(128)S(1)}, s32[16]{0:T(128)}, u32[]{:S(2)}) copy-start(s32[16]{0:T(128)} %param.26) | copy-start | bytes 196
  0.8 41.2 %copy-start.1 = (bf16[4,3584]{1,0:T(4,128)(2,1)S(1)}, bf16[4,3584]{1,0:T(4,128)(2,1)}, u32[]{:S(2)}) copy-start(bf16[4,3584]{1,0:T(4,128)(2,1)} %param.15) | copy-start | bytes 86020
  0.8 41.3 %copy-start.3 = (f32[3584]{0:T(1024)S(1)}, f32[3584]{0:T(1024)}, u32[]{:S(2)}) copy-start(f32[3584]{0:T(1024)} %param.23) | copy-start | bytes 43012
  0.8 46.3 %copy-start.5 = (f32[4,8]{1,0:T(4,128)S(1)}, f32[4,8]{1,0:T(4,128)}, u32[]{:S(2)}) copy-start(f32[4,8]{1,0:T(4,128)} %param.25) | copy-start | bytes 388
  9.4 14.3 %all-to-all-start = ((bf16[4,16,512]{2,0,1:T(4,128)(2,1)}), bf16[4,16,512]{2,0,1:T(4,128)(2,1)S(1)}, u32[]{:S(2)}, u32[]{:S(2)}) async-start(bf16[4,16,512]{2,0,1:T(4,128)(2,1)} %copy.23), calls=%async_computation | async-start | bytes 131072 | tf_op jit(solution)/shard_map/all_to_all | solution.py:51
  25.0 16.8 %all-to-all-start.1 = ((bf16[16,4,3584]{2,1,0:T(4,128)(2,1)}), bf16[16,4,3584]{2,1,0:T(4,128)(2,1)S(1)}, u32[]{:S(2)}, u32[]{:S(2)}) async-start(bf16[16,4,3584]{2,1,0:T(4,128)(2,1)} %reshape.61), calls=%async_computation.1 | async-start | bytes 917504 | tf_op jit(solution)/shard_map/all_to_all | solution.py:69
  43.3 13.3 %all-to-all-start.2 = ((bf16[16,2,3584]{2,1,0:T(2,128)(2,1)}), bf16[16,2,3584]{2,1,0:T(2,128)(2,1)S(1)}, u32[]{:S(2)}, u32[]{:S(2)}) async-start(bf16[16,2,3584]{2,1,0:T(2,128)(2,1)} %copy.24), calls=%async_computation.2 | async-start | bytes 458752 | tf_op jit(solution)/shard_map/all_to_all | solution.py:76
  71.5 13.0 %all-to-all-start.3 = ((bf16[16,2,3584]{2,1,0:T(2,128)(2,1)}), bf16[16,2,3584]{2,1,0:T(2,128)(2,1)S(1)}, u32[]{:S(2)}, u32[]{:S(2)}) async-start(bf16[16,2,3584]{2,1,0:T(2,128)(2,1)} %convert_element_type.63), calls=%async_computation.3 | async-start | bytes 458752 | tf_op jit(solution)/shard_map/all_to_all | solution.py:85

commit v2 on v1

v2 whole, which is shorter than its diff:
```python
import functools

import jax
import jax.numpy as jnp
from jax import lax
from jax.experimental import pallas as pl
from jax.experimental.pallas import tpu as pltpu
from jax.sharding import PartitionSpec as P

F32 = jnp.float32
BF16 = jnp.bfloat16
NT = (((1,), (1,)), ((), ()))


def kernel(
    devices,
    rows_dev,
    heads_dev,
    cap,
    parts,
    scale,
    lengths_ref,
    q_latent,
    q_rope,
    resid,
    gain,
    spread,
    gather,
    cache_latent_hbm,
    cache_rope_hbm,
    w_value_hbm,
    w_out_hbm,
    w_gate_hbm,
    w_up_hbm,
    w_down_hbm,
    out,
    cache_latent,
    cache_rope,
    w_value,
    w_out,
    w_gate,
    w_up,
    w_down,
    o_wide,
    o_send,
    o_recv,
    p_wide,
    p_send,
    p_recv,
    n_send,
    n_recv,
    n_wide,
    e_wide,
    e_send,
    e_recv,
    act,
    load_sem,
    send_sem,
    recv_sem,
):
    me = lax.axis_index("ep")
    group = lax.axis_index("groups")
    loads = []
    for r in range(rows_dev):
        loads.append((cache_latent_hbm.at[r], cache_latent.at[r]))
        loads.append((cache_rope_hbm.at[r], cache_rope.at[r]))
    loads += [
        (w_value_hbm, w_value),
        (w_out_hbm, w_out),
        (w_gate_hbm, w_gate),
        (w_up_hbm, w_up),
        (w_down_hbm, w_down),
    ]
    loads = [pltpu.make_async_copy(a, b, load_sem.at[i]) for i, (a, b) in enumerate(loads)]
    for load in loads:
        load.start()

    barrier = pltpu.get_barrier_semaphore()

    @pl.loop(1, devices)
    def _(k):
        peer = lax.rem(me + k, devices)
        pl.semaphore_signal(
            barrier, inc=1, device_id=(group, peer), device_id_type=pl.DeviceIdType.MESH
        )

    def copy(phase, k, src, dst, to):
        return pltpu.make_async_remote_copy(
            src_ref=src.at[to],
            dst_ref=dst.at[me],
            send_sem=send_sem.at[phase, k],
            recv_sem=recv_sem.at[phase, k],
            device_id=(group, to),
            device_id_type=pl.DeviceIdType.MESH,
        )

    def send_all(phase, src, dst):
        @pl.loop(1, devices)
        def _(k):
            copy(phase, k, src, dst, lax.rem(me + k, devices)).start()

        dst[me] = src[me]

    def recv_all(phase, src, dst):
        @pl.loop(1, devices)
        def _(k):
            copy(phase, k, src, dst, lax.rem(me + k, devices)).wait_recv()

    def sent_all(phase, src, dst):
        @pl.loop(1, devices)
        def _(k):
            copy(phase, k, src, dst, lax.rem(me + k, devices)).wait_send()

    length, lat = cache_latent.shape[1:]
    heads = q_latent.shape[1]
    pos = lax.broadcasted_iota(jnp.int32, (heads, length), 1)
    for r in range(rows_dev):
        loads[2 * r].wait()
        loads[2 * r + 1].wait()
        keys = cache_latent[r]
        scores = lax.dot_general(q_latent[r], keys, NT, preferred_element_type=F32)
        scores = scores + jnp.dot(q_rope[r], cache_rope[r], preferred_element_type=F32)
        valid = pos < lengths_ref[r]
        scores = jnp.where(valid, scores * scale, -1e30)
        top = jnp.max(scores, axis=-1, keepdims=True)
        expo = jnp.where(valid, jnp.exp(scores - top), 0.0)
        probs = (expo / jnp.sum(expo, axis=-1, keepdims=True)).astype(BF16)
        o = jnp.dot(probs, keys, preferred_element_type=F32)
        for c in range(lat // 128):
            o_wide[:, r * (lat // 128) + c, :] = o[:, c * 128 : (c + 1) * 128]
    o_send[...] = o_wide[...].astype(BF16)
    pl.semaphore_wait(barrier, devices - 1)
    send_all(0, o_send, o_recv)

    loads[2 * rows_dev].wait()
    loads[2 * rows_dev + 1].wait()
    recv_all(0, o_send, o_recv)
    o_wide[...] = o_recv[...].astype(F32)
    steps = lat // 128
    o_all = jnp.concatenate(
        [
            jnp.concatenate([o_wide[:, r * steps + c, :] for c in range(steps)], axis=1)
            for r in range(rows_dev)
        ],
        axis=0,
    ).astype(BF16)
    values = jnp.dot(o_all, w_value[0], preferred_element_type=F32).astype(BF16)
    width = w_out.shape[1]
    piece = width // parts
    for q in range(parts):
        partial = jnp.dot(
            values, w_out[:, q * piece : (q + 1) * piece], preferred_element_type=F32
        )
        for r in range(rows_dev):
            p_wide[:, r * parts + q, :] = partial[r * devices : (r + 1) * devices, :]
    p_send[...] = p_wide[...].astype(BF16)
    send_all(1, p_send, p_recv)
    recv_all(1, p_send, p_recv)
    hidden = lax.fori_loop(
        0, devices, lambda d, total: total + p_recv[d].astype(F32), resid[...].astype(F32)
    )

    count = rows_dev * parts
    same = (
        lax.broadcasted_iota(jnp.int32, (count, count), 0) // parts
        == lax.broadcasted_iota(jnp.int32, (count, count), 1) // parts
    ).astype(F32)
    square = jnp.dot(
        same, hidden * hidden, precision=lax.Precision.HIGHEST, preferred_element_type=F32
    )
    mean_sq = jnp.sum(square, axis=-1, keepdims=True) / width
    normed = (hidden * lax.rsqrt(mean_sq + 1e-06) * gain[...]).astype(BF16)
    slot = cap * parts
    outgoing = jnp.dot(spread[...], normed, preferred_element_type=F32)
    n_send[...] = outgoing.reshape(devices, slot, piece).astype(BF16)
    send_all(2, n_send, n_recv)

    loads[2 * rows_dev + 2].wait()
    loads[2 * rows_dev + 3].wait()
    recv_all(2, n_send, n_recv)
    n_wide[...] = n_recv[...].astype(F32)
    taken = jnp.concatenate(
        [
            jnp.concatenate([n_wide[:, c * parts + q, :] for q in range(parts)], axis=1)
            for c in range(cap)
        ],
        axis=0,
    ).astype(BF16)
    units = w_gate.shape[0]
    block = min(units, 256)
    for b in range(units // block):
        at = slice(b * block, (b + 1) * block)
        gate = lax.dot_general(taken, w_gate[at, :], NT, preferred_element_type=F32)
        up = lax.dot_general(taken, w_up[at, :], NT, preferred_element_type=F32)
        act[:, at] = (gate / (1.0 + jnp.exp(-gate)) * up).astype(BF16)
    loads[2 * rows_dev + 4].wait()
    for q in range(parts):
        part = jnp.dot(act[...], w_down[:, q * piece : (q + 1) * piece], preferred_element_type=F32)
        for c in range(cap):
            e_wide[:, c * parts + q, :] = part[c * devices : (c + 1) * devices, :]
    e_send[...] = e_wide[...].astype(BF16)
    send_all(3, e_send, e_recv)
    recv_all(3, e_send, e_recv)
    returned = e_recv[...].astype(F32).reshape(devices * slot, piece)
    moe = jnp.dot(
        gather[...], returned, precision=lax.Precision.HIGHEST, preferred_element_type=F32
    )
    out[...] = (hidden + moe).astype(BF16)
    sent_all(0, o_send, o_recv)
    sent_all(1, p_send, p_recv)
    sent_all(2, n_send, n_recv)
    sent_all(3, e_send, e_recv)


def local(
    resid,
    q_latent,
    q_rope,
    cache_latent,
    cache_rope,
    lengths,
    w_value,
    w_out,
    norm_gain,
    routes,
    route_scores,
    placement,
    w_gate,
    w_up,
    w_down,
):
    devices = lax.axis_size("ep")
    rows_dev, width = resid.shape
    heads_dev, lat, vhead = w_value.shape
    experts = placement.shape[0]
    top_count = routes.shape[1]
    cap = rows_dev * top_count // experts
    shards = devices // experts
    scale = (vhead + q_rope.shape[2]) ** (-0.5)
    parts = 16 // rows_dev
    piece = width // parts
    assert heads_dev == 1 and piece % 128 == 0

    expert_ids = jnp.arange(experts, dtype=jnp.int32)
    slot_of_dev = jnp.arange(devices, dtype=jnp.int32) // shards
    dev_expert = (placement[None, :] == slot_of_dev[:, None])
    weights = 2.5 * route_scores / jnp.sum(route_scores, axis=-1, keepdims=True)
    held = jnp.any(
        (routes[:, :, None, None] == expert_ids[None, None, None, :]) & dev_expert[None, None],
        axis=3,
    )
    member = jnp.any(held, axis=1)
    weight_dev = jnp.sum(jnp.where(held, weights[:, :, None], 0.0), axis=1)
    count = member.astype(jnp.int32)
    rank = jnp.sum(
        jnp.where(
            jnp.arange(rows_dev)[:, None, None] > jnp.arange(rows_dev)[None, :, None],
            count[None],
            0,
        ),
        axis=1,
    )
    pick = member[:, :, None] & (rank[:, :, None] == jnp.arange(cap)[None, None, :])
    same = jnp.eye(parts, dtype=jnp.bool_)
    full = pick[:, None, :, :, None] & same[None, :, None, None, :]
    slot = cap * parts
    gather = jnp.where(full, weight_dev[:, None, :, None, None], 0.0).reshape(
        rows_dev * parts, devices * slot
    )
    spread = jnp.transpose(full, (2, 3, 4, 0, 1)).astype(BF16).reshape(
        devices * slot, rows_dev * parts
    )
    gain = jnp.tile(norm_gain.reshape(parts, piece), (rows_dev, 1))

    any_spec = pl.BlockSpec(memory_space=pl.ANY)
    vmem = pl.BlockSpec(memory_space=pltpu.VMEM)
    scratch = [
        pltpu.VMEM(a.shape, a.dtype)
        for a in (cache_latent, cache_rope, w_value, w_out, w_gate, w_up, w_down)
    ]
    steps = rows_dev * (lat // 128)
    o_shape = (devices, steps, 128)
    p_shape = (devices, rows_dev * parts, piece)
    n_shape = (devices, slot, piece)
    scratch += [pltpu.VMEM(o_shape, t) for t in (F32, BF16, BF16)]
    scratch += [pltpu.VMEM(p_shape, t) for t in (F32, BF16, BF16)]
    scratch += [pltpu.VMEM(n_shape, t) for t in (BF16, BF16, F32, F32, BF16, BF16)]
    scratch += [
        pltpu.VMEM((cap * devices, w_gate.shape[0]), BF16),
        pltpu.SemaphoreType.DMA((2 * rows_dev + 5,)),
        pltpu.SemaphoreType.DMA((4, devices)),
        pltpu.SemaphoreType.DMA((4, devices)),
    ]
    out = pl.pallas_call(
        functools.partial(kernel, devices, rows_dev, heads_dev, cap, parts, scale),
        out_shape=jax.ShapeDtypeStruct((rows_dev * parts, piece), BF16),
        in_specs=[pl.BlockSpec(memory_space=pltpu.SMEM)] + [vmem] * 6 + [any_spec] * 7,
        out_specs=vmem,
        scratch_shapes=scratch,
        compiler_params=pltpu.CompilerParams(
            collective_id=0, has_side_effects=True, vmem_limit_bytes=56 * 1024 * 1024
        ),
    )(
        lengths,
        q_latent,
        q_rope,
        resid.reshape(rows_dev * parts, piece),
        gain,
        spread,
        gather,
        cache_latent,
        cache_rope,
        w_value,
        w_out,
        w_gate,
        w_up,
        w_down,
    )
    return out.reshape(rows_dev, width)


def solution(mesh):
    ep = ("groups", "ep")
    return jax.shard_map(
        local,
        mesh=mesh,
        in_specs=(
            P(ep, None),
            P(ep, None, None),
            P(ep, None, None),
            P(ep, None, None),
            P(ep, None, None),
            P(ep),
            P("ep", None, None),
            P("ep", None),
            P(),
            P(ep, None),
            P(ep, None),
            P("groups"),
            P("ep", None),
            P("ep", None),
            P("ep", None),
        ),
        out_specs=P(ep, None),
        check_vma=False,
    )
```

time: 86 us -> 57.2 us (0.67)
  Pallas kernels: 0 us -> 46.4 us
  waiting for transfers between devices: 38.4 us -> 0 us
  matrix products: 23.4 us -> 0 us
  starting transfers between devices: 18.3 us -> 0 us
  other arithmetic: 1.82 us -> 4.44 us
  local copies, waits for them, and re-layouts: 3.38 us -> 5.96 us
    pallas_call x0 -> x1, Pallas kernels: none -> 46.4 us  [local(): pl.pallas_call(functools.partial(kernel, devices, rows_dev, heads_dev, ca...]
    all_to_all x4 -> x0, waiting for transfers between devices: 38.4 us -> none  [the longest x1 13 us: local(): lax.all_to_all(partial, 'ep', split_axis=0, concat_axis=0, tiled=True)]
    dot_general x9 -> x0, matrix products: 23.3 us -> none  [the longest x1 8.69 us: local(): jnp.dot(act, w_down, preferred_element_type=jnp.float32)]
    all_to_all x4 -> x0, starting transfers between devices: 18.3 us -> none  [the longest x1 7.39 us: local(): lax.all_to_all(o_local, 'ep', split_axis=1, concat_axis=0, tiled=True)]
    reshape x2, local copies, waits for them, and re-layouts: 0.97 us -> 2.75 us  [the longest x1 1.38 us: local(): resid.reshape(rows_dev * parts, piece)]
    convert_element_type x3 -> x2, local copies, waits for them, and re-layouts: 2.36 us -> 0.9 us  [local(): jnp.transpose(full, (2, 3, 4, 0, 1)).astype(BF16)]
    eq x1 -> x4, other arithmetic: 0.01 us -> 1.43 us  [the longest x1 0.75 us: local(): routes[:, :, None, None] == expert_ids[None, None, None, :]]
    another operation x1 -> x3, local copies, waits for them, and re-layouts: 0.02 us -> 1.38 us  [local(): gain = jnp.tile(norm_gain.reshape(parts, piece), (rows_dev, 1))]
  transfers between devices with their start and end apart: 4 -> 0, of which waited for: 4 -> 0; matrix products, arithmetic and copies ran while one was open for 1% -> 0% of each run, Pallas kernels for 0% -> 0%
where the time goes in v2:
time: 57.2 us; the launch traced here: 56.8 us
  Pallas kernels  46.4 us (81%)
  local copies, waits for them, and re-layouts  5.96 us (10%)
  other arithmetic  4.44 us (8%)
    pallas_call x1, Pallas kernels, local(): pl.pallas_call(functools.partial(kernel, devices, rows_dev, heads_dev, ca...  46.4 us
    reshape x1, local copies, waits for them, and re-layouts, local(): resid.reshape(rows_dev * parts, piece)  1.38 us
    another operation x3, local copies, waits for them, and re-layouts, local(): gain = jnp.tile(norm_gain.reshape(parts, piece), (rows_dev, 1))  1.38 us
    reshape x1, local copies, waits for them, and re-layouts, local(): return out.reshape(rows_dev, width)  1.37 us

profile of v2, /device:TPU:0, one launch (start us, length us, event | category | flops | bytes accessed | tf_op | source)
XLA Modules:
  0.0 56.8 jit_solution(502936991495558660)
XLA Ops:
  0.0 0.8 %iota_compare_fusion.2 = pred[4,8,16]{2,1,0:T(8,128)(4,1)S(1)} fusion(s32[4,8]{1,0:T(4,128)} %param.24), kind=kLoop, calls=%fused_computation.9 | loop fusion | flops 512 | bytes 640 | tf_op jit(solution)/shard_map/eq | solution.py:249
  0.8 0.7 %iota_compare_fusion.3 = pred[16,16]{1,0:T(8,128)(4,1)S(1)} fusion(s32[16]{0:T(128)} %param.26), kind=kLoop, calls=%fused_computation.11 | loop fusion | flops 256 | bytes 320 | tf_op jit(solution)/shard_map/eq | solution.py:246
  1.4 0.7 %and_reduce_fusion = (pred[4,8,16]{2,1,0:T(8,128)(4,1)S(1)}, pred[4,16]{1,0:T(4,128)(4,1)S(1)}) fusion(pred[16,16]{1,0:T(8,128)(4,1)S(1)} %iota_compare_fusion.3, pred[4,8,16]{2,1,0:T(8,128)(4,1)S(1)} %iota_compare_fusion.2), kind=kLoop, calls=%fused_computation.2 | loop fusion | flops 24000 | bytes 1344 | tf_op jit(solution)/shard_map/reduce_or | solution.py:248
  2.1 0.1 select_reduce_fusion.1
  2.2 0.1 fusion.1
  2.3 0.8 %reduce_sum.28 = f32[4]{0:T(128)S(1)} reduce(f32[4,8]{1,0:T(4,128)} %param.25, f32[]{:T(128)} %constant.18.clone.1), dimensions={1}, to_apply=%region_3.4 | reduce | flops 28 | bytes 148 | tf_op jit(solution)/shard_map/reduce_sum | solution.py:247
  3.1 0.8 %multiply_divide_fusion = f32[4,8]{1,0:T(4,128)S(1)} fusion(f32[4,8]{1,0:T(4,128)} %param.25, f32[4]{0:T(128)S(1)} %reduce_sum.28), kind=kLoop, calls=%fused_computation.12 | loop fusion | flops 64 | bytes 272 | tf_op jit(solution)/shard_map/div | solution.py:247
  3.9 0.1 select_reduce_fusion
  4.0 0.2 and_select_fusion
  4.2 0.9 %select_n.23.gather = f32[16,128]{1,0:T(8,128)} reshape(f32[4,4,16,2,4]{4,3,2,1,0:T(2,128)S(1)} %and_select_fusion) | data formatting | bytes 16384 | tf_op jit(solution)/shard_map/jit(_where)/select_n | solution.py:267
  5.1 0.1 fusion
  5.2 0.2 and_convert_fusion
  5.4 0.2 reshape.93
  5.6 0.7 %copy.19.spread = bf16[128,16]{1,0:T(8,128)(2,1)} copy(bf16[128,16]{0,1:T(8,128)(2,1)S(1)} %reshape.93) | data formatting | bytes 8192 | tf_op jit(solution)/shard_map/convert_element_type | solution.py:270
  6.3 0.7 %tile.10 = f32[4,896]{1,0:T(4,128)S(1)} reshape(f32[3584]{0:T(1024)} %param.23) | data formatting | bytes 28672 | tf_op jit(solution)/shard_map/tile | solution.py:273
  7.1 0.6 %tile.12.gain = f32[16,896]{1,0:T(8,128)} reshape(f32[4,4,896]{2,1,0:T(4,128)S(1)} %tile.11) | data formatting | bytes 114688 | tf_op jit(solution)/shard_map/tile | solution.py:273
  7.7 1.4 %reshape.91.resid = bf16[16,896]{1,0:T(8,128)(2,1)} reshape(bf16[4,3584]{1,0:T(4,128)(2,1)} %param.15) | data formatting | bytes 57344 | tf_op jit(solution)/shard_map/reshape | solution.py:307
  9.1 46.4 %shard_map.145 = bf16[16,896]{1,0:T(8,128)(2,1)} custom-call(s32[4]{0:T(128)} %lengths_ref.1, bf16[4,16,512]{2,1,0:T(8,128)(2,1)} %q_latent.1, bf16[4,16,64]{2,1,0:T(8,128)(2,1)} %q_rope.1, bf16[16,896]{1,0:T(8,128)(2,1)} %reshape.91.resid, f32[16,896]{1,0:T(8,128)} %tile.12.gain, bf16[128,16]{1,0:T(8,128)(2,1)} %copy.19.spread, f32[16,128]{1,0:T(8,128)} %select_n.23.gather, ...), custom_call_target="tpu_custom_call" | custom-call | tf_op jit(solution)/shard_map/pallas_call | solution.py:294
  55.4 1.4 %reshape.92 = bf16[4,3584]{1,0:T(4,128)(2,1)} reshape(bf16[16,896]{1,0:T(8,128)(2,1)} %shard_map.145) | data formatting | bytes 57344 | tf_op jit(solution)/shard_map/reshape | solution.py:319
  (5 shorter events, 0.0 us)

commit v3 on v2

--- a/solution.py
+++ b/solution.py
@@ -15,17 +15,18 @@
 def kernel(
     devices,
     rows_dev,
-    heads_dev,
     cap,
     parts,
+    shards,
     scale,
     lengths_ref,
+    routes_ref,
+    scores_ref,
+    placement_ref,
     q_latent,
     q_rope,
     resid,
-    gain,
-    spread,
-    gather,
+    norm_gain,
     cache_latent_hbm,
     cache_rope_hbm,
     w_value_hbm,
@@ -54,6 +55,9 @@
     e_send,
     e_recv,
     act,
+    hidden_wide,
+    gain,
+    final,
     load_sem,
     send_sem,
     recv_sem,
@@ -132,6 +136,38 @@
     pl.semaphore_wait(barrier, devices - 1)
     send_all(0, o_send, o_recv)
 
+    width = w_out.shape[1]
+    piece = width // parts
+    slot = cap * parts
+    wide = resid[...].astype(F32)
+    for r in range(rows_dev):
+        for q in range(parts):
+            at = slice(q * piece, (q + 1) * piece)
+            hidden_wide[r * parts + q : r * parts + q + 1, :] = wide[r : r + 1, at]
+            gain[r * parts + q : r * parts + q + 1, :] = norm_gain[:, at]
+
+    count = rows_dev * parts
+    lane = lax.broadcasted_iota(jnp.int32, (count, devices * slot), 1)
+    line = lax.broadcasted_iota(jnp.int32, (count, devices * slot), 0)
+    row = line // parts
+    holder = lane // (slot * shards)
+    member = jnp.zeros(lane.shape, F32)
+    rank = jnp.zeros(lane.shape, F32)
+    score = jnp.zeros(lane.shape, F32)
+    score_sum = jnp.zeros(lane.shape, F32)
+    for r in range(rows_dev):
+        for k in range(routes_ref.shape[1]):
+            named = holder == placement_ref[routes_ref[r, k]]
+            own = named & (row == r)
+            member = member + jnp.where(own, 1.0, 0.0)
+            rank = rank + jnp.where(named & (row > r), 1.0, 0.0)
+            score = score + jnp.where(own, scores_ref[r, k], 0.0)
+            score_sum = score_sum + jnp.where(row == r, scores_ref[r, k], 0.0)
+    choice = lax.rem(lane // parts, cap).astype(F32)
+    pick = (member > 0.5) & (rank == choice) & (lax.rem(lane, parts) == lax.rem(line, parts))
+    gather = jnp.where(pick, 2.5 * score / score_sum, 0.0)
+    spread = jnp.where(pick, 1.0, 0.0).T.astype(BF16)
+
     loads[2 * rows_dev].wait()
     loads[2 * rows_dev + 1].wait()
     recv_all(0, o_send, o_recv)
@@ -145,8 +181,6 @@
         axis=0,
     ).astype(BF16)
     values = jnp.dot(o_all, w_value[0], preferred_element_type=F32).astype(BF16)
-    width = w_out.shape[1]
-    piece = width // parts
     for q in range(parts):
         partial = jnp.dot(
             values, w_out[:, q * piece : (q + 1) * piece], preferred_element_type=F32
@@ -157,10 +191,9 @@
     send_all(1, p_send, p_recv)
     recv_all(1, p_send, p_recv)
     hidden = lax.fori_loop(
-        0, devices, lambda d, total: total + p_recv[d].astype(F32), resid[...].astype(F32)
-    )
-
-    count = rows_dev * parts
+        0, devices, lambda d, total: total + p_recv[d].astype(F32), hidden_wide[...]
+    )
+
     same = (
         lax.broadcasted_iota(jnp.int32, (count, count), 0) // parts
         == lax.broadcasted_iota(jnp.int32, (count, count), 1) // parts
@@ -170,8 +203,7 @@
     )
     mean_sq = jnp.sum(square, axis=-1, keepdims=True) / width
     normed = (hidden * lax.rsqrt(mean_sq + 1e-06) * gain[...]).astype(BF16)
-    slot = cap * parts
-    outgoing = jnp.dot(spread[...], normed, preferred_element_type=F32)
+    outgoing = jnp.dot(spread, normed, preferred_element_type=F32)
     n_send[...] = outgoing.reshape(devices, slot, piece).astype(BF16)
     send_all(2, n_send, n_recv)
 
@@ -203,9 +235,13 @@
     recv_all(3, e_send, e_recv)
     returned = e_recv[...].astype(F32).reshape(devices * slot, piece)
     moe = jnp.dot(
-        gather[...], returned, precision=lax.Precision.HIGHEST, preferred_element_type=F32
-    )
-    out[...] = (hidden + moe).astype(BF16)
+        gather, returned, precision=lax.Precision.HIGHEST, preferred_element_type=F32
+    )
+    mixed = hidden + moe
+    for r in range(rows_dev):
+        for q in range(parts):
+            final[r : r + 1, q * piece : (q + 1) * piece] = mixed[r * parts + q : r * parts + q + 1, :]
+    out[...] = final[...].astype(BF16)
     sent_all(0, o_send, o_recv)
     sent_all(1, p_send, p_recv)
     sent_all(2, n_send, n_recv)
@@ -241,37 +277,7 @@
     piece = width // parts
     assert heads_dev == 1 and piece % 128 == 0
 
-    expert_ids = jnp.arange(experts, dtype=jnp.int32)
-    slot_of_dev = jnp.arange(devices, dtype=jnp.int32) // shards
-    dev_expert = (placement[None, :] == slot_of_dev[:, None])
-    weights = 2.5 * route_scores / jnp.sum(route_scores, axis=-1, keepdims=True)
-    held = jnp.any(
-        (routes[:, :, None, None] == expert_ids[None, None, None, :]) & dev_expert[None, None],
-        axis=3,
-    )
-    member = jnp.any(held, axis=1)
-    weight_dev = jnp.sum(jnp.where(held, weights[:, :, None], 0.0), axis=1)
-    count = member.astype(jnp.int32)
-    rank = jnp.sum(
-        jnp.where(
-            jnp.arange(rows_dev)[:, None, None] > jnp.arange(rows_dev)[None, :, None],
-            count[None],
-            0,
-        ),
-        axis=1,
-    )
-    pick = member[:, :, None] & (rank[:, :, None] == jnp.arange(cap)[None, None, :])
-    same = jnp.eye(parts, dtype=jnp.bool_)
-    full = pick[:, None, :, :, None] & same[None, :, None, None, :]
     slot = cap * parts
-    gather = jnp.where(full, weight_dev[:, None, :, None, None], 0.0).reshape(
-        rows_dev * parts, devices * slot
-    )
-    spread = jnp.transpose(full, (2, 3, 4, 0, 1)).astype(BF16).reshape(
-        devices * slot, rows_dev * parts
-    )
-    gain = jnp.tile(norm_gain.reshape(parts, piece), (rows_dev, 1))
-
     any_spec = pl.BlockSpec(memory_space=pl.ANY)
     vmem = pl.BlockSpec(memory_space=pltpu.VMEM)
     scratch = [
@@ -287,14 +293,17 @@
     scratch += [pltpu.VMEM(n_shape, t) for t in (BF16, BF16, F32, F32, BF16, BF16)]
     scratch += [
         pltpu.VMEM((cap * devices, w_gate.shape[0]), BF16),
+        pltpu.VMEM((rows_dev * parts, piece), F32),
+        pltpu.VMEM((rows_dev * parts, piece), F32),
+        pltpu.VMEM((rows_dev, width), F32),
         pltpu.SemaphoreType.DMA((2 * rows_dev + 5,)),
         pltpu.SemaphoreType.DMA((4, devices)),
         pltpu.SemaphoreType.DMA((4, devices)),
     ]
     out = pl.pallas_call(
-        functools.partial(kernel, devices, rows_dev, heads_dev, cap, parts, scale),
-        out_shape=jax.ShapeDtypeStruct((rows_dev * parts, piece), BF16),
-        in_specs=[pl.BlockSpec(memory_space=pltpu.SMEM)] + [vmem] * 6 + [any_spec] * 7,
+        functools.partial(kernel, devices, rows_dev, cap, parts, shards, scale),
+        out_shape=jax.ShapeDtypeStruct((rows_dev, width), BF16),
+        in_specs=[pl.BlockSpec(memory_space=pltpu.SMEM)] * 4 + [vmem] * 4 + [any_spec] * 7,
         out_specs=vmem,
         scratch_shapes=scratch,
         compiler_params=pltpu.CompilerParams(
@@ -302,12 +311,13 @@
         ),
     )(
         lengths,
+        routes,
+        route_scores,
+        placement,
         q_latent,
         q_rope,
-        resid.reshape(rows_dev * parts, piece),
-        gain,
-        spread,
-        gather,
+        resid,
+        norm_gain.reshape(1, width),
         cache_latent,
         cache_rope,
         w_value,
@@ -316,7 +326,7 @@
         w_up,
         w_down,
     )
-    return out.reshape(rows_dev, width)
+    return out
 
 
 def solution(mesh):

time: 57.2 us -> 49.3 us (0.86)
  other arithmetic: 4.44 us -> 0 us
  local copies, waits for them, and re-layouts: 5.96 us -> 2.69 us
    eq x4 -> x0, other arithmetic: 1.43 us -> none  [the longest x1 0.75 us: local(): routes[:, :, None, None] == expert_ids[None, None, None, :]]
    reshape x2 -> x1, local copies, waits for them, and re-layouts: 2.75 us -> 1.33 us  [local(): norm_gain.reshape(1, width)]
    another operation x3 -> x0, local copies, waits for them, and re-layouts: 1.38 us -> none  [local(): gain = jnp.tile(norm_gain.reshape(parts, piece), (rows_dev, 1))]
    unnamed x0 -> x1, local copies, waits for them, and re-layouts: none -> 1.37 us
    reduce_sum x3 -> x0, other arithmetic: 0.98 us -> none  [the longest x1 0.8 us: local(): weights = 2.5 * route_scores / jnp.sum(route_scores, axis=-1, keepdims=True)]
    select_n x1 -> x0, local copies, waits for them, and re-layouts: 0.93 us -> none  [local(): jnp.where(full, weight_dev[:, None, :, None, None], 0.0)]
    convert_element_type x2 -> x0, local copies, waits for them, and re-layouts: 0.9 us -> none  [local(): jnp.transpose(full, (2, 3, 4, 0, 1)).astype(BF16)]
    div x1 -> x0, other arithmetic: 0.75 us -> none  [local(): weights = 2.5 * route_scores / jnp.sum(route_scores, axis=-1, keepdims=True)]
where the time goes in v3:
time: 49.3 us; the launch traced here: 49.1 us
  Pallas kernels  46.3 us (94%)
  local copies, waits for them, and re-layouts  2.69 us (5%)
    pallas_call x1, Pallas kernels, local(): pl.pallas_call(functools.partial(kernel, devices, rows_dev, cap, parts, s...  46.3 us
    unnamed x1, local copies, waits for them, and re-layouts  1.37 us
    reshape x1, local copies, waits for them, and re-layouts, local(): norm_gain.reshape(1, width)  1.33 us

profile of v3, /device:TPU:0, one launch (start us, length us, event | category | flops | bytes accessed | tf_op | source)
XLA Modules:
  0.0 49.1 jit_solution(15653562947104811048)
XLA Ops:
  0.0 1.3 %reshape.3.norm_gain = f32[1,3584]{1,0:T(1,128)} reshape(f32[3584]{0:T(1024)} %param.23) | data formatting | bytes 28672 | tf_op jit(solution)/shard_map/reshape | solution.py:320
  1.3 46.3 %shard_map.145 = bf16[4,3584]{1,0:T(4,128)(2,1)} custom-call(s32[4]{0:T(128)} %lengths_ref.1, s32[4,8]{1,0:T(4,128)} %routes_ref.1, f32[4,8]{1,0:T(4,128)} %scores_ref.1, s32[16]{0:T(128)} %placement_ref.1, bf16[4,16,512]{2,1,0:T(8,128)(2,1)} %q_latent.1, bf16[4,16,64]{2,1,0:T(8,128)(2,1)} %q_rope.1, bf16[4,3584]{1,0:T(4,128)(2,1)} %resid.1, ...), custom_call_target="tpu_custom_call" | custom-call | tf_op jit(solution)/shard_map/pallas_call | solution.py:303
  47.7 1.4 %copy.17 = bf16[4,3584]{1,0:T(4,128)(2,1)} copy(bf16[4,3584]{1,0:T(4,128)(2,1)} %shard_map.145) | data formatting | bytes 57344

commit v4 on v3

--- a/solution.py
+++ b/solution.py
@@ -47,6 +47,8 @@
     o_recv,
     p_wide,
     p_send,
+    q_recv,
+    s_send,
     p_recv,
     n_send,
     n_recv,
@@ -76,44 +78,68 @@
         (w_down_hbm, w_down),
     ]
     loads = [pltpu.make_async_copy(a, b, load_sem.at[i]) for i, (a, b) in enumerate(loads)]
-    for load in loads:
+    early = 2 * rows_dev + 2
+    for load in loads[:early]:
         load.start()
 
     barrier = pltpu.get_barrier_semaphore()
+
+    chips = devices // 2
+    core = lax.rem(me, 2)
+    chip = me // 2
+
+    def peer_of(k):
+        peer, bit = 0, 1
+        while bit < devices:
+            mine, other = lax.rem(me // bit, 2), lax.rem(k // bit, 2)
+            peer = peer + bit * (mine + other - 2 * mine * other)
+            bit *= 2
+        return peer
 
     @pl.loop(1, devices)
     def _(k):
-        peer = lax.rem(me + k, devices)
         pl.semaphore_signal(
-            barrier, inc=1, device_id=(group, peer), device_id_type=pl.DeviceIdType.MESH
+            barrier, inc=1, device_id=(group, peer_of(k)), device_id_type=pl.DeviceIdType.MESH
         )
 
     def copy(phase, k, src, dst, to):
         return pltpu.make_async_remote_copy(
-            src_ref=src.at[to],
-            dst_ref=dst.at[me],
+            src_ref=src,
+            dst_ref=dst,
             send_sem=send_sem.at[phase, k],
             recv_sem=recv_sem.at[phase, k],
             device_id=(group, to),
             device_id_type=pl.DeviceIdType.MESH,
         )
 
-    def send_all(phase, src, dst):
-        @pl.loop(1, devices)
-        def _(k):
-            copy(phase, k, src, dst, lax.rem(me + k, devices)).start()
-
-        dst[me] = src[me]
-
-    def recv_all(phase, src, dst):
-        @pl.loop(1, devices)
-        def _(k):
-            copy(phase, k, src, dst, lax.rem(me + k, devices)).wait_recv()
-
-    def sent_all(phase, src, dst):
-        @pl.loop(1, devices)
-        def _(k):
-            copy(phase, k, src, dst, lax.rem(me + k, devices)).wait_send()
+    by_core = core * chips + chip
+
+    def exchange(phase, act_on):
+        @pl.loop(0, (chips if phase == 1 else devices) - 1)
+        def _(j):
+            if phase == 1:
+                k = devices - 2 - 2 * j
+            else:
+                k = devices - 1 - j
+            to = peer_of(k)
+            if phase == 0:
+                pair = o_send.at[to], o_recv.at[by_core]
+            elif phase == 1:
+                pair = s_send.at[to // 2], p_recv.at[chip]
+            elif phase == 2:
+                pair = n_send.at[to], n_recv.at[me]
+            else:
+                pair = e_send.at[to], e_recv.at[me]
+            act_on(copy(phase, k, *pair, to))
+
+    def send_all(phase):
+        exchange(phase, lambda c: c.start())
+
+    def recv_all(phase):
+        exchange(phase, lambda c: c.wait_recv())
+
+    def sent_all(phase):
+        exchange(phase, lambda c: c.wait_send())
 
     length, lat = cache_latent.shape[1:]
     heads = q_latent.shape[1]
@@ -121,6 +147,9 @@
     for r in range(rows_dev):
         loads[2 * r].wait()
         loads[2 * r + 1].wait()
+        if r == rows_dev - 1:
+            for load in loads[early:]:
+                load.start()
         keys = cache_latent[r]
         scores = lax.dot_general(q_latent[r], keys, NT, preferred_element_type=F32)
         scores = scores + jnp.dot(q_rope[r], cache_rope[r], preferred_element_type=F32)
@@ -134,7 +163,8 @@
             o_wide[:, r * (lat // 128) + c, :] = o[:, c * 128 : (c + 1) * 128]
     o_send[...] = o_wide[...].astype(BF16)
     pl.semaphore_wait(barrier, devices - 1)
-    send_all(0, o_send, o_recv)
+    send_all(0)
+    o_recv[by_core] = o_send[me]
 
     width = w_out.shape[1]
     piece = width // parts
@@ -170,7 +200,7 @@
 
     loads[2 * rows_dev].wait()
     loads[2 * rows_dev + 1].wait()
-    recv_all(0, o_send, o_recv)
+    recv_all(0)
     o_wide[...] = o_recv[...].astype(F32)
     steps = lat // 128
     o_all = jnp.concatenate(
@@ -187,11 +217,20 @@
         )
         for r in range(rows_dev):
             p_wide[:, r * parts + q, :] = partial[r * devices : (r + 1) * devices, :]
-    p_send[...] = p_wide[...].astype(BF16)
-    send_all(1, p_send, p_recv)
-    recv_all(1, p_send, p_recv)
+    p_send[...] = p_wide[pl.ds((1 - core) * chips, chips)].astype(BF16)
+    swap = copy(4, 1, p_send, q_recv, me + 1 - 2 * core)
+    swap.start()
+    swap.wait_recv()
+
+    @pl.loop(0, chips)
+    def _(c):
+        s_send[c] = (p_wide[core * chips + c] + q_recv[c].astype(F32)).astype(BF16)
+
+    send_all(1)
+    p_recv[chip] = s_send[chip]
+    recv_all(1)
     hidden = lax.fori_loop(
-        0, devices, lambda d, total: total + p_recv[d].astype(F32), hidden_wide[...]
+        0, chips, lambda d, total: total + p_recv[d].astype(F32), hidden_wide[...]
     )
 
     same = (
@@ -205,11 +244,12 @@
     normed = (hidden * lax.rsqrt(mean_sq + 1e-06) * gain[...]).astype(BF16)
     outgoing = jnp.dot(spread, normed, preferred_element_type=F32)
     n_send[...] = outgoing.reshape(devices, slot, piece).astype(BF16)
-    send_all(2, n_send, n_recv)
+    send_all(2)
+    n_recv[me] = n_send[me]
 
     loads[2 * rows_dev + 2].wait()
     loads[2 * rows_dev + 3].wait()
-    recv_all(2, n_send, n_recv)
+    recv_all(2)
     n_wide[...] = n_recv[...].astype(F32)
     taken = jnp.concatenate(
         [
@@ -231,8 +271,9 @@
         for c in range(cap):
             e_wide[:, c * parts + q, :] = part[c * devices : (c + 1) * devices, :]
     e_send[...] = e_wide[...].astype(BF16)
-    send_all(3, e_send, e_recv)
-    recv_all(3, e_send, e_recv)
+    send_all(3)
+    e_recv[me] = e_send[me]
+    recv_all(3)
     returned = e_recv[...].astype(F32).reshape(devices * slot, piece)
     moe = jnp.dot(
         gather, returned, precision=lax.Precision.HIGHEST, preferred_element_type=F32
@@ -242,10 +283,9 @@
         for q in range(parts):
             final[r : r + 1, q * piece : (q + 1) * piece] = mixed[r * parts + q : r * parts + q + 1, :]
     out[...] = final[...].astype(BF16)
-    sent_all(0, o_send, o_recv)
-    sent_all(1, p_send, p_recv)
-    sent_all(2, n_send, n_recv)
-    sent_all(3, e_send, e_recv)
+    swap.wait_send()
+    for phase in range(4):
+        sent_all(phase)
 
 
 def local(
@@ -275,7 +315,7 @@
     scale = (vhead + q_rope.shape[2]) ** (-0.5)
     parts = 16 // rows_dev
     piece = width // parts
-    assert heads_dev == 1 and piece % 128 == 0
+    assert heads_dev == 1 and piece % 128 == 0 and devices & (devices - 1) == 0
 
     slot = cap * parts
     any_spec = pl.BlockSpec(memory_space=pl.ANY)
@@ -289,7 +329,8 @@
     p_shape = (devices, rows_dev * parts, piece)
     n_shape = (devices, slot, piece)
     scratch += [pltpu.VMEM(o_shape, t) for t in (F32, BF16, BF16)]
-    scratch += [pltpu.VMEM(p_shape, t) for t in (F32, BF16, BF16)]
+    scratch += [pltpu.VMEM(p_shape, F32)]
+    scratch += [pltpu.VMEM((devices // 2,) + p_shape[1:], BF16)] * 4
     scratch += [pltpu.VMEM(n_shape, t) for t in (BF16, BF16, F32, F32, BF16, BF16)]
     scratch += [
         pltpu.VMEM((cap * devices, w_gate.shape[0]), BF16),
@@ -297,8 +338,8 @@
         pltpu.VMEM((rows_dev * parts, piece), F32),
         pltpu.VMEM((rows_dev, width), F32),
         pltpu.SemaphoreType.DMA((2 * rows_dev + 5,)),
-        pltpu.SemaphoreType.DMA((4, devices)),
-        pltpu.SemaphoreType.DMA((4, devices)),
+        pltpu.SemaphoreType.DMA((5, devices)),
+        pltpu.SemaphoreType.DMA((5, devices)),
     ]
     out = pl.pallas_call(
         functools.partial(kernel, devices, rows_dev, cap, parts, shards, scale),

time: 49.3 us -> 47.5 us (0.963)
  Pallas kernels: 46.3 us -> 44.5 us
    pallas_call x1, Pallas kernels: 46.3 us -> 44.5 us  [local(): pl.pallas_call(functools.partial(kernel, devices, rows_dev, cap, parts, s...]
where the time goes in v4:
time: 47.5 us; the launch traced here: 47.2 us
  Pallas kernels  44.5 us (94%)
  local copies, waits for them, and re-layouts  2.69 us (6%)
    pallas_call x1, Pallas kernels, local(): pl.pallas_call(functools.partial(kernel, devices, rows_dev, cap, parts, s...  44.5 us
    unnamed x1, local copies, waits for them, and re-layouts  1.37 us
    reshape x1, local copies, waits for them, and re-layouts, local(): norm_gain.reshape(1, width)  1.33 us

profile of v4, /device:TPU:0, one launch (start us, length us, event | category | flops | bytes accessed | tf_op | source)
XLA Modules:
  0.0 47.2 jit_solution(6535574244231654386)
XLA Ops:
  0.0 1.3 %reshape.3.norm_gain = f32[1,3584]{1,0:T(1,128)} reshape(f32[3584]{0:T(1024)} %param.23) | data formatting | bytes 28672 | tf_op jit(solution)/shard_map/reshape | solution.py:361
  1.3 44.5 %shard_map.145 = bf16[4,3584]{1,0:T(4,128)(2,1)} custom-call(s32[4]{0:T(128)} %lengths_ref.1, s32[4,8]{1,0:T(4,128)} %routes_ref.1, f32[4,8]{1,0:T(4,128)} %scores_ref.1, s32[16]{0:T(128)} %placement_ref.1, bf16[4,16,512]{2,1,0:T(8,128)(2,1)} %q_latent.1, bf16[4,16,64]{2,1,0:T(8,128)(2,1)} %q_rope.1, bf16[4,3584]{1,0:T(4,128)(2,1)} %resid.1, ...), custom_call_target="tpu_custom_call" | custom-call | tf_op jit(solution)/shard_map/pallas_call | solution.py:344
  45.8 1.4 %copy.17 = bf16[4,3584]{1,0:T(4,128)(2,1)} copy(bf16[4,3584]{1,0:T(4,128)(2,1)} %shard_map.145) | data formatting | bytes 57344

commit v5 on v4

--- a/solution.py
+++ b/solution.py
@@ -114,8 +114,8 @@
 
     by_core = core * chips + chip
 
-    def exchange(phase, act_on):
-        @pl.loop(0, (chips if phase == 1 else devices) - 1)
+    def exchange(phase, act_on, make=None):
+        @pl.loop(0, (chips if phase == 1 else devices) - 1, unroll=devices <= 16)
         def _(j):
             if phase == 1:
                 k = devices - 2 - 2 * j
@@ -130,10 +130,13 @@
                 pair = n_send.at[to], n_recv.at[me]
             else:
                 pair = e_send.at[to], e_recv.at[me]
+            if make is not None:
+                make(to // 2 if phase == 1 else to)
             act_on(copy(phase, k, *pair, to))
 
-    def send_all(phase):
-        exchange(phase, lambda c: c.start())
+    def send_all(phase, make):
+        exchange(phase, lambda c: c.start(), make)
+        make(chip if phase == 1 else me)
 
     def recv_all(phase):
         exchange(phase, lambda c: c.wait_recv())
@@ -161,9 +164,12 @@
         o = jnp.dot(probs, keys, preferred_element_type=F32)
         for c in range(lat // 128):
             o_wide[:, r * (lat // 128) + c, :] = o[:, c * 128 : (c + 1) * 128]
-    o_send[...] = o_wide[...].astype(BF16)
+
+    def make_o(d):
+        o_send[d] = o_wide[d].astype(BF16)
+
     pl.semaphore_wait(barrier, devices - 1)
-    send_all(0)
+    send_all(0, make_o)
     o_recv[by_core] = o_send[me]
 
     width = w_out.shape[1]
@@ -222,11 +228,10 @@
     swap.start()
     swap.wait_recv()
 
-    @pl.loop(0, chips)
-    def _(c):
+    def make_s(c):
         s_send[c] = (p_wide[core * chips + c] + q_recv[c].astype(F32)).astype(BF16)
 
-    send_all(1)
+    send_all(1, make_s)
     p_recv[chip] = s_send[chip]
     recv_all(1)
     hidden = lax.fori_loop(
@@ -243,8 +248,12 @@
     mean_sq = jnp.sum(square, axis=-1, keepdims=True) / width
     normed = (hidden * lax.rsqrt(mean_sq + 1e-06) * gain[...]).astype(BF16)
     outgoing = jnp.dot(spread, normed, preferred_element_type=F32)
-    n_send[...] = outgoing.reshape(devices, slot, piece).astype(BF16)
-    send_all(2)
+    n_wide[...] = outgoing.reshape(devices, slot, piece)
+
+    def make_n(d):
+        n_send[d] = n_wide[d].astype(BF16)
+
+    send_all(2, make_n)
     n_recv[me] = n_send[me]
 
     loads[2 * rows_dev + 2].wait()
@@ -270,8 +279,11 @@
         part = jnp.dot(act[...], w_down[:, q * piece : (q + 1) * piece], preferred_element_type=F32)
         for c in range(cap):
             e_wide[:, c * parts + q, :] = part[c * devices : (c + 1) * devices, :]
-    e_send[...] = e_wide[...].astype(BF16)
-    send_all(3)
+
+    def make_e(d):
+        e_send[d] = e_wide[d].astype(BF16)
+
+    send_all(3, make_e)
     e_recv[me] = e_send[me]
     recv_all(3)
     returned = e_recv[...].astype(F32).reshape(devices * slot, piece)

time: 47.5 us -> 46.9 us (0.987)
  Pallas kernels: 44.5 us -> 44 us
    pallas_call x1, Pallas kernels: 44.5 us -> 44 us  [local(): pl.pallas_call(functools.partial(kernel, devices, rows_dev, cap, parts, s...]
where the time goes in v5:
time: 46.9 us; the launch traced here: 46.7 us
  Pallas kernels  44 us (94%)
  local copies, waits for them, and re-layouts  2.69 us (6%)
    pallas_call x1, Pallas kernels, local(): pl.pallas_call(functools.partial(kernel, devices, rows_dev, cap, parts, s...  44 us
    unnamed x1, local copies, waits for them, and re-layouts  1.37 us
    reshape x1, local copies, waits for them, and re-layouts, local(): norm_gain.reshape(1, width)  1.33 us

profile of v5, /device:TPU:0, one launch (start us, length us, event | category | flops | bytes accessed | tf_op | source)
XLA Modules:
  0.0 46.7 jit_solution(14405666781201565113)
XLA Ops:
  0.0 1.3 %reshape.3.norm_gain = f32[1,3584]{1,0:T(1,128)} reshape(f32[3584]{0:T(1024)} %param.23) | data formatting | bytes 28672 | tf_op jit(solution)/shard_map/reshape | solution.py:373
  1.3 44.0 %shard_map.145 = bf16[4,3584]{1,0:T(4,128)(2,1)} custom-call(s32[4]{0:T(128)} %lengths_ref.1, s32[4,8]{1,0:T(4,128)} %routes_ref.1, f32[4,8]{1,0:T(4,128)} %scores_ref.1, s32[16]{0:T(128)} %placement_ref.1, bf16[4,16,512]{2,1,0:T(8,128)(2,1)} %q_latent.1, bf16[4,16,64]{2,1,0:T(8,128)(2,1)} %q_rope.1, bf16[4,3584]{1,0:T(4,128)(2,1)} %resid.1, ...), custom_call_target="tpu_custom_call" | custom-call | tf_op jit(solution)/shard_map/pallas_call | solution.py:356
  45.3 1.4 %copy.17 = bf16[4,3584]{1,0:T(4,128)(2,1)} copy(bf16[4,3584]{1,0:T(4,128)(2,1)} %shard_map.145) | data formatting | bytes 57344
